TPU v7x, 32 devices: a whole 2x2x4 slice. The times are simulated.
32 devices in a mesh: policy: 4 (over y, x), zero: 8 (over z, core).
Axes of the slice: x: 2, y: 2, z: 4, core: 2. Of those that a mesh axis runs over, the one named last changes fastest.
Arguments:
- acts: bfloat16 [4, 5120, 4608], P('policy', 'zero'), may hold values from -6 to 6
- cotan: bfloat16 [4, 5120, 1024], P('policy', 'zero'), may hold values from -6 to 6
- advantage: int32 [4, 40], P('policy', 'zero'), may hold values from -4 to 4
- merge_ratio: int32 [4], replicated, may hold values from 1 to 8
- weight: bfloat16 [4, 4608, 1024], P('policy', 'zero'), may hold values from -0.3125 to 0.3125
- anchor: float32 [4, 4608, 1024], P('policy', 'zero'), may hold values from -0.3125 to 0.3125
- init: bfloat16 [4608, 1024], P('zero'), may hold values from -0.62 to 0.62
Outputs:
- anchor_new: float32 [4, 4608, 1024], P('policy', 'zero')
- merged: bfloat16 [4608, 1024], P('zero')
- merged_out: float32 [4, 5120, 1024], P('policy', 'zero')
All inputs are finite; a program needn't handle non-finite values.
Results may differ from a plain program's by a relative error of at most 0.015.
Values may be sent and summed in bfloat16 or wider, within the bound.
A program may use at most 128 MiB of HBM per device.

v0:
```python
import math

import jax
import jax.numpy as jnp
from jax import lax
from jax.sharding import PartitionSpec as P

SEQ = 128


step_size = 0.02
ema_decay = 0.9


def on_device(acts, cotan, advantage, merge_ratio, weight, anchor, init):
    acts_local = acts[0]
    tok_local = acts_local.shape[0]
    seq_count = advantage.shape[1]
    levels = advantage[0].astype(jnp.float32) * 0.25
    scaled = (
        (cotan[0].astype(jnp.float32).reshape(seq_count, SEQ, -1) * levels[:, None, None])
        .reshape(tok_local, -1)
        .astype(jnp.bfloat16)
    )
    grad = lax.psum_scatter(
        lax.dot_general(
            acts_local, scaled, (((0,), (0,)), ((), ())), preferred_element_type=jnp.float32
        ).astype(jnp.bfloat16),
        "zero",
        scatter_dimension=0,
        tiled=True,
    ).astype(jnp.float32)
    total_tokens = tok_local * lax.axis_size("zero")
    updated = weight[0].astype(jnp.float32) - step_size * grad / math.sqrt(total_tokens)
    anchor_new = ema_decay * anchor[0] + (1.0 - ema_decay) * updated
    task = updated - init.astype(jnp.float32)
    norm_sq = lax.psum(jnp.sum(task * task), "zero")
    ratio = merge_ratio.astype(jnp.float32)
    share = ratio[lax.axis_index("policy")] / jnp.sum(ratio)
    target = lax.psum(share * jnp.sqrt(norm_sq), "policy")
    term = share * task
    mixed = lax.psum(term, "policy")
    mixed_sq = lax.psum(jnp.sum(mixed * mixed), "zero")
    merged = (init.astype(jnp.float32) + mixed * (target / jnp.sqrt(mixed_sq))).astype(jnp.bfloat16)
    result = jnp.dot(
        acts_local,
        lax.all_gather(merged, "zero", axis=0, tiled=True),
        preferred_element_type=jnp.float32,
    )
    return (anchor_new[None], merged, result[None])


def solution(mesh):
    placed = (
        P("policy", "zero", None),
        P("policy", "zero", None),
        P("policy", "zero"),
        P(),
        P("policy", "zero", None),
        P("policy", "zero", None),
        P("zero", None),
    )
    return jax.shard_map(
        on_device,
        mesh=mesh,
        in_specs=placed,
        out_specs=(P("policy", "zero", None), P("zero", None), P("policy", "zero", None)),
        check_vma=False,
    )
```

profile of v0, /device:TPU:0, one launch (start us, length us, event | category | flops | bytes accessed | tf_op | source)
XLA Modules:
  0.0 365.8 jit_solution(5771478485958375912)
XLA Ops:
  7.2 0.0 reduce-scatter.4.cloned.1.call-start
  7.2 0.7 multiply_bitcast_fusion
  7.9 0.1 broadcast_bitcast_fusion
  7.9 12.4 %fusion = bf16[4608,1024]{0,1:T(8,128)(2,1)} fusion(bf16[1,640,4608]{2,1,0:T(8,128)(2,1)} %param.7, bf16[1,640,1024]{2,1,0:T(8,128)(2,1)} %param.8, f32[640]{0:T(1024)S(1)} %broadcast_bitcast_fusion), kind=kOutput, calls=%fused_computation.1 | convolution fusion | flops 6046482432 | bytes 16648704 | tf_op jit(solution)/shard_map/dot_general | solution.py:26
  20.3 12.7 %copy.23 = bf16[4608,1024]{1,0:T(8,128)(2,1)} copy(bf16[4608,1024]{0,1:T(8,128)(2,1)} %fusion) | data formatting | bytes 18874368
  33.0 0.0 reduce-scatter.4.cloned.1.call-update
  33.0 0.0 copy-start.2
  33.0 0.0 all-reduce.3.cloned.1.call-start
  33.1 1.2 copy-done.1
  34.3 0.7 copy.18
  35.0 1.7 copy.17
  36.7 0.0 copy-done.2
  36.7 3.2 copy.16
  39.9 0.6 dynamic_slice.3
  40.5 0.6 convert_reduce_fusion
  42.4 93.0 %reduce-scatter.4.cloned.1.call-done = bf16[576,1024]{1,0:T(8,128)(2,1)} async-done(((bf16[4608,1024]{1,0:T(8,128)(2,1)}), bf16[576,1024]{1,0:T(8,128)(2,1)}) %reduce-scatter.4.cloned.1.call-update) | async-done | bytes 1179664
  135.4 2.4 copy.24
  137.8 6.1 %multiply_reduce_fusion.1 = (f32[]{:T(128)}, f32[576,1024]{0,1:T(8,128)}, f32[1,576,1024]{1,2,0:T(8,128)}) fusion(bf16[576,1024]{0,1:T(8,128)(2,1)S(1)} %copy.18, bf16[576,1024]{0,1:T(8,128)(2,1)} %copy.24, bf16[1,576,1024]{1,2,0:T(8,128)(2,1)S(1)} %copy.17, f32[]{:T(128)S(6)} %div.14, f32[1,576,1024]{1,2,0:T(8,128)} %copy.16), kind=kLoop, calls=%fused_computation.12 | loop fusion | flops 7077887 | bytes 10616840 | tf_op jit(solution)/shard_map/reduce_sum | solution.py:37
  143.9 0.0 all-reduce.3.cloned.1.call-update
  143.9 0.0 all-gather.2.cloned.1.call-start
  144.0 76.8 %all-reduce.3.cloned.1.call-done = f32[576,1024]{0,1:T(8,128)} async-done(((f32[576,1024]{0,1:T(8,128)}), f32[576,1024]{0,1:T(8,128)}) %all-reduce.3.cloned.1.call-update) | async-done | bytes 2359312 | tf_op jit(solution)/shard_map/psum | solution.py:42
  220.8 3.0 multiply_reduce_fusion
  223.8 17.0 %all-reduce = (f32[]{:T(128)}, f32[]{:T(128)}) all-reduce(f32[]{:T(128)} %get-tuple-element.11, f32[]{:T(128)} %multiply_reduce_fusion), channel_id=1, replica_groups=mesh['policy'=4,'zero'=8] {'zero'}, use_global_device_ids=true, to_apply=%region_4.0 | all-reduce | flops 2 | bytes 16 | tf_op jit(solution)/shard_map/psum | solution.py:37
  241.5 9.6 %psum.30 = f32[]{:T(128)} all-reduce(f32[]{:T(128)S(6)} %mul.76), channel_id=1, replica_groups=mesh['policy'=4,'zero'=8] {'policy'}, use_global_device_ids=true, to_apply=%region_5.0 | all-reduce | flops 1 | bytes 8 | tf_op jit(solution)/shard_map/psum | solution.py:40
  252.4 3.1 fusion.4
  255.5 2.5 copy.21
  258.0 0.0 all-gather.2.cloned.1.call-update
  258.1 0.0 copy-done
  258.1 2.0 copy.20
  260.1 86.1 %all-gather.2.cloned.1.call-done = bf16[4608,1024]{1,0:T(8,128)(2,1)} async-done(((bf16[576,1024]{1,0:T(8,128)(2,1)}), bf16[4608,1024]{1,0:T(8,128)(2,1)}) %all-gather.2.cloned.1.call-update) | async-done | bytes 9437200 | tf_op jit(solution)/shard_map/all_gather | solution.py:47
  346.2 11.0 %fusion.6 = f32[1,640,1024]{1,2,0:T(8,128)S(1)} fusion(bf16[4608,1024]{1,0:T(8,128)(2,1)} %all-gather.2.cloned.1.call-done, bf16[1,640,4608]{2,1,0:T(8,128)(2,1)} %param.7), kind=kOutput, calls=%fused_computation.14 | convolution fusion | flops 6039797760 | bytes 17956864 | tf_op jit(solution)/shard_map/dot_general | solution.py:45
  357.2 2.1 copy.22
  (3 shorter events, 0.0 us)
Async XLA Ops:
  7.2 128.3 %reduce-scatter.4.cloned.1.call-start = ((), (), s32[]{:S(2)}) async-start(), calls=%async_computation.3 | async-start | bytes 10616832
  33.0 1.3 copy-start.1
  33.0 3.7 copy-start.2
  33.0 187.7 %all-reduce.3.cloned.1.call-start = ((), (), s32[]{:S(2)}) async-start(), calls=%async_computation.1 | async-start | bytes 5242880 | tf_op jit(solution)/shard_map/psum | solution.py:42
  143.9 202.2 %all-gather.2.cloned.1.call-start = ((), (), s32[]{:S(2)}) async-start(), calls=%async_computation.2 | async-start | bytes 10616832 | tf_op jit(solution)/shard_map/all_gather | solution.py:47
  255.5 2.5 copy-start
Sparse Core Ops, SparseCore 0:
  33.2 102.2 reduce-scatter.3
  144.1 76.6 all-reduce.2
  258.2 87.9 all-gather.1
where the time goes:
time: 367 us; the launch traced here: 366 us
  waiting for transfers between devices  256 us (70%)
  local copies, waits for them, and re-layouts  29.1 us (8%)
  blocking collectives  26.6 us (7%)
  matrix products  23.4 us (6%)
  between operations  17.2 us (5%)
  other arithmetic  13.5 us (4%)
    unnamed x4, waiting for transfers between devices  93 us
    all_gather x1, waiting for transfers between devices, on_device(): lax.all_gather(merged, 'zero', axis=0, tiled=True)  86.1 us
    psum x1, waiting for transfers between devices, on_device(): mixed = lax.psum(term, 'policy')  76.8 us
    unnamed x14, local copies, waits for them, and re-layouts  28.5 us
    psum x1, blocking collectives, on_device(): norm_sq = lax.psum(jnp.sum(task * task), 'zero')  17 us
    dot_general x1, matrix products, on_device(): lax.dot_general(acts_local, scaled, (((0,), (0,)), ((), ())), preferred_e...  12.4 us
    dot_general x1, matrix products, on_device(): jnp.dot(acts_local, lax.all_gather(merged, 'zero', axis=0, tiled=True), p...  11 us
    psum x1, blocking collectives, on_device(): target = lax.psum(share * jnp.sqrt(norm_sq), 'policy')  9.62 us
  transfers between devices with their start and end apart: 3, of which 3 were waited for; matrix products, arithmetic and copies ran while one was open for 2% of the time, Pallas kernels for 0%

commit v1 on v0

v1 whole, which is shorter than its diff:
```python
import functools
import math

import jax
import jax.numpy as jnp
from jax import lax
from jax.experimental import pallas as pl
from jax.experimental.pallas import tpu as pltpu
from jax.sharding import PartitionSpec as P

SEQ = 128
STEP = 0.02
DECAY = 0.9
CHUNKS = 3
SUB = 16
F32 = jnp.float32
BF16 = jnp.bfloat16
MESH = pl.DeviceIdType.MESH


def flip(index, mask):
    out, bit = 0, 1
    while bit <= mask:
        digit = (index // bit) % 2
        out = out + bit * ((1 - digit) if mask & bit else digit)
        bit *= 2
    return out + (index // bit) * bit


def remote(src, dst, send, recv, **where):
    return pltpu.make_async_remote_copy(
        src_ref=src, dst_ref=dst, send_sem=send, recv_sem=recv, device_id=where, device_id_type=MESH
    )


def kernel(
    n_pol, n_zero, total_tokens,
    acts, cotan, adv, ratio, weight, anchor, init,
    anchor_out, merged_out, result,
    scaled, part, sib, up, dn, grad, ubuf, prec, mixed, mg, nsq, msq, ztile, ptile,
    sib_s, sib_r, up_s, up_r, dn_s, dn_r, pol_s, pol_r, zs_s, zs_r, ps_s, ps_r, ag_r, line_s, peer_s, core_s, relay_s,
):
    p = lax.axis_index("policy")
    b = lax.axis_index("zero")
    z, c = b // 2, b % 2
    nz = n_zero // 2
    rows, width = init.shape
    depth = acts.shape[1]
    pair = 2 * rows
    cw = width // n_pol
    R = rows // CHUNKS
    other = b + 1 - 2 * c
    sends = []

    def post(cond, make):
        @pl.when(cond)
        def _():
            make().start()
        sends.append((cond, make))

    barrier = pltpu.get_barrier_semaphore()
    for j in range(1, n_zero):
        pl.semaphore_signal(barrier, inc=1, device_id={"zero": lax.rem(b + j, n_zero)}, device_id_type=MESH)
    for j in range(1, n_pol):
        pl.semaphore_signal(barrier, inc=1, device_id={"policy": flip(p, j)}, device_id_type=MESH)

    for s in range(adv.shape[1]):
        level = adv[0, s].astype(F32) * 0.25

        @pl.loop(0, SEQ // SUB)
        def _(i):
            at = pl.ds(pl.multiple_of(s * SEQ + i * SUB, SUB), SUB)
            scaled[at, :] = (cotan[at, :].astype(F32) * level).astype(BF16)

    nsq[...] = jnp.zeros_like(nsq)
    msq[...] = jnp.zeros_like(msq)
    pl.semaphore_wait(barrier, n_zero - 1 + n_pol - 1)

    T = 384

    def tiles(first, count):
        @pl.loop(0, count)
        def _(j):
            at = pl.ds(pl.multiple_of(first + j * T, 128), T)
            part[at, :] = lax.dot_general(
                acts[:, at], scaled[...], (((0,), (0,)), ((), ())), preferred_element_type=F32
            ).astype(BF16)

    def to_sibling(d):
        def make():
            src = part.at[pl.ds(pl.multiple_of(d * pair + (1 - c) * rows, 16), rows), :]
            return remote(src, sib.at[d], sib_s.at[d], sib_r.at[d], zero=other)
        make().start()
        sends.append((None, make))

    order = []
    for i in range((nz + 1) // 2):
        order += [nz - 1 - i] + ([i] if i != nz - 1 - i else [])
    if pair % T == 0:
        for d in order:
            tiles(d * pair, pair // T)
            to_sibling(d)
    else:
        tiles(0, depth // T)
        for d in order:
            to_sibling(d)

    def sib_wait(d):
        remote(sib.at[d], sib.at[d], sib_s.at[d], sib_r.at[d], zero=other).wait_recv()

    def relay(k):
        for i in range(nz - 1):
            for (d, here, end, first_, recv, r_sem, s_sem, slot, step) in (
                (nz - 1 - i, z < nz - 1 - i, z == 0, 0, up, up_r, up_s, nz - 2 - i, 2),
                (i, z > i, z == nz - 1, nz - 1, dn, dn_r, dn_s, i, -2),
            ):
                mine = pl.ds(k * R, R)

                def make(d=d, recv=recv, r_sem=r_sem, s_sem=s_sem, slot=slot, step=step, k=k, i=i, mine=mine):
                    src = part.at[pl.ds(pl.multiple_of(d * pair + c * rows + k * R, 16), R), :]
                    return remote(
                        src, recv.at[slot, mine, :], s_sem.at[slot, k], r_sem.at[slot, k], zero=b + step
                    )

                def add(with_recv, d=d, recv=recv, slot=slot):
                    @pl.loop(0, R // SUB)
                    def _(t):
                        own = pl.ds(pl.multiple_of(d * pair + c * rows + k * R + t * SUB, SUB), SUB)
                        at = pl.ds(pl.multiple_of(k * R + t * SUB, SUB), SUB)
                        acc = part[own, :].astype(F32) + sib[d, at, :].astype(F32)
                        if with_recv:
                            acc = acc + recv[slot, at, :].astype(F32)
                        part[own, :] = acc.astype(BF16)

                if k == 0:
                    @pl.when(here)
                    def _():
                        sib_wait(d)

                @pl.when(jnp.logical_and(here, end))
                def _():
                    add(False)

                @pl.when(jnp.logical_and(here, jnp.logical_not(end)))
                def _():
                    remote(
                        recv.at[slot, mine, :], recv.at[slot, mine, :], s_sem.at[slot, k], r_sem.at[slot, k], zero=b
                    ).wait_recv()
                    add(True)

                post(here, make)

    share = jnp.full((8, 128), ratio[p].astype(F32), F32)
    whole = 0
    for q in range(n_pol):
        whole = whole + ratio[q]
    whole = jnp.full((8, 128), whole.astype(F32), F32)
    share = (share / whole)[0:1, 0:1]
    factor = STEP / math.sqrt(total_tokens)

    def final(k):
        mine = pl.ds(k * R, R)
        if k == 0:
            sib_wait(z)

        @pl.when(z > 0)
        def _():
            slot = z - 1
            remote(up.at[slot, mine, :], up.at[slot, mine, :], up_s.at[slot, k], up_r.at[slot, k], zero=b).wait_recv()

        @pl.when(z < nz - 1)
        def _():
            remote(dn.at[z, mine, :], dn.at[z, mine, :], dn_s.at[z, k], dn_r.at[z, k], zero=b).wait_recv()

        @pl.loop(0, R // SUB)
        def _(t):
            at = pl.ds(pl.multiple_of(k * R + t * SUB, SUB), SUB)
            own = pl.ds(pl.multiple_of(b * rows + k * R + t * SUB, SUB), SUB)
            grad[...] = part[own, :].astype(F32) + sib[z, at, :].astype(F32)

            @pl.when(z > 0)
            def _():
                grad[...] += up[z - 1, at, :].astype(F32)

            @pl.when(z < nz - 1)
            def _():
                grad[...] += dn[z, at, :].astype(F32)

            updated = weight[at, :].astype(F32) - factor * grad[...]
            anchor_out[at, :] = DECAY * anchor[at, :] + (1.0 - DECAY) * updated
            task = updated - init[at, :].astype(F32)
            sq = task * task
            nsq[...] += sq[:8] + sq[8:]
            term = (share * updated).astype(BF16)
            for q in range(n_pol):
                ubuf[q, at, :] = term[:, q * cw:(q + 1) * cw]

        for j in range(1, n_pol):
            def make(j=j):
                q = flip(p, j)
                return remote(
                    ubuf.at[q, mine, :], prec.at[j - 1, mine, :], pol_s.at[j - 1, k], pol_r.at[j - 1, k], policy=q
                )
            make().start()
            sends.append((None, make))

    columns = pl.ds(pl.multiple_of(p * cw, 128), cw)

    def mix(k):
        mine = pl.ds(k * R, R)
        for j in range(1, n_pol):
            ref = prec.at[j - 1, mine, :]
            remote(ref, ref, pol_s.at[j - 1, k], pol_r.at[j - 1, k], policy=p).wait_recv()

        @pl.loop(0, R // SUB)
        def _(t):
            at = pl.ds(pl.multiple_of(k * R + t * SUB, SUB), SUB)
            acc = ubuf[p, at, :].astype(F32)
            for j in range(1, n_pol):
                acc = acc + prec[j - 1, at, :].astype(F32)
            acc = acc - init[at, columns].astype(F32)
            mixed[at, :] = acc
            sq = acc * acc
            msq[...] += sq[:8] + sq[8:]

    for k in range(CHUNKS):
        relay(k)
        if k >= 1:
            final(k - 1)
        if k >= 2:
            mix(k - 2)
    final(CHUNKS - 1)
    for k in range(max(CHUNKS - 2, 0), CHUNKS):
        mix(k)

    ztile[b, 0] = jnp.full((8, 128), jnp.sum(nsq[...]), F32)
    ztile[b, 1] = jnp.full((8, 128), jnp.sum(msq[...]), F32)
    for j in range(1, n_zero):
        def make(j=j):
            return remote(ztile.at[b], ztile.at[b], zs_s.at[j], zs_r.at[j], zero=lax.rem(b + j, n_zero))
        make().start()
        sends.append((None, make))
    result[...] = jnp.zeros_like(result)
    for j in range(1, n_zero):
        ref = ztile.at[lax.rem(b + n_zero - j, n_zero)]
        remote(ref, ref, zs_s.at[j], zs_r.at[j], zero=b).wait_recv()
    ptile[p, 0] = jnp.sum(ztile[:, 0], axis=0)
    ptile[p, 1] = jnp.sum(ztile[:, 1], axis=0)
    for j in range(1, n_pol):
        def make(j=j):
            return remote(ptile.at[p], ptile.at[p], ps_s.at[j], ps_r.at[j], policy=flip(p, j))
        make().start()
        sends.append((None, make))
    for j in range(1, n_pol):
        ref = ptile.at[flip(p, j)]
        remote(ref, ref, ps_s.at[j], ps_r.at[j], policy=p).wait_recv()
    target = jnp.zeros((8, 128), F32)
    mixed_sq = jnp.zeros((8, 128), F32)
    for q in range(n_pol):
        target = target + jnp.full((8, 128), ratio[q].astype(F32), F32) / whole * jnp.sqrt(ptile[q, 0])
        mixed_sq = mixed_sq + ptile[q, 1]
    scale = (target / jnp.sqrt(mixed_sq))[0:1, 0:1]

    @pl.loop(0, rows // SUB)
    def _(t):
        at = pl.ds(pl.multiple_of(t * SUB, SUB), SUB)
        own = pl.ds(pl.multiple_of(b * rows + t * SUB, SUB), SUB)
        mg[p, own, :] = (init[at, columns].astype(F32) + mixed[at, :] * scale).astype(BF16)

    square = n_pol == 4
    direct = (1, 2) if square else tuple(range(1, n_pol))
    half = rows // 2

    def piece(q, block):
        return mg.at[q, pl.ds(pl.multiple_of(block * rows, 16), rows), :]

    def halves(q, block, h):
        return mg.at[q, pl.ds(pl.multiple_of(block * rows + h * half, 16), half), :]

    def arrived(ref, sem):
        remote(ref, ref, sem, sem, zero=b).wait_recv()

    def offsets(t):
        if t < 0 or t >= nz:
            return []
        return [0] if t == 0 else [-t, t]

    def valid(o):
        return jnp.logical_and(z + o >= 0, z + o < nz)

    def stage_line(t):
        for o in offsets(t):
            ok = valid(o)
            zz = z + o
            bb = 2 * zz + c
            if t:
                @pl.when(ok)
                def _():
                    arrived(piece(p, bb), ag_r.at[0, bb])
            if o <= 0:
                post(jnp.logical_and(ok, z < nz - 1), lambda zz=zz, bb=bb: remote(
                    piece(p, bb), piece(p, bb), line_s.at[0, zz], ag_r.at[0, bb], zero=b + 2))
            if o >= 0:
                post(jnp.logical_and(ok, z > 0), lambda zz=zz, bb=bb: remote(
                    piece(p, bb), piece(p, bb), line_s.at[1, zz], ag_r.at[0, bb], zero=b - 2))
            for j in direct:
                post(ok, lambda zz=zz, bb=bb, j=j: remote(
                    piece(p, bb), piece(p, bb), peer_s.at[j, zz], ag_r.at[j, bb], policy=flip(p, j)))
            post(ok, lambda zz=zz, bb=bb: remote(
                piece(p, bb), piece(p, bb), core_s.at[0, zz], ag_r.at[0, bb], zero=other))

    def stage_peer(t):
        for o in offsets(t):
            ok = valid(o)
            zz = z + o
            bb = 2 * zz + c
            for j in direct:
                q = flip(p, j)

                @pl.when(ok)
                def _(j=j, q=q):
                    arrived(piece(q, bb), ag_r.at[j, bb])
                if square:
                    post(ok, lambda zz=zz, bb=bb, j=j, q=q: remote(
                        halves(q, bb, j - 1), halves(q, bb, j - 1), relay_s.at[j - 1, zz], ag_r.at[2 + j, bb],
                        policy=flip(p, 3 - j)))
                post(ok, lambda zz=zz, bb=bb, j=j, q=q: remote(
                    piece(q, bb), piece(q, bb), core_s.at[j, zz], ag_r.at[j, bb], zero=other))

    def stage_diagonal(t):
        if not square:
            return
        for o in offsets(t):
            ok = valid(o)
            zz = z + o
            bb = 2 * zz + c
            q = flip(p, 3)
            for h in (0, 1):
                @pl.when(ok)
                def _(h=h):
                    arrived(halves(q, bb, h), ag_r.at[3 + h, bb])
                post(ok, lambda zz=zz, bb=bb, h=h, q=q: remote(
                    halves(q, bb, h), halves(q, bb, h), core_s.at[3 + h, zz], ag_r.at[3 + h, bb], zero=other))

    def multiply(first, count):
        k_at = pl.ds(pl.multiple_of(first, 128), count)

        @pl.loop(0, n_pol)
        def _(q):
            n_at = pl.ds(pl.multiple_of(q * cw, 128), cw)
            result[:, n_at] += jnp.dot(acts[:, k_at], mg[q, k_at, :], preferred_element_type=F32)

    def stage_multiply(t):
        for o in offsets(t):
            zz = z + o
            bs = 2 * zz + 1 - c

            @pl.when(valid(o))
            def _():
                arrived(piece(p, bs), ag_r.at[0, bs])
                for j in direct:
                    arrived(piece(flip(p, j), bs), ag_r.at[j, bs])
                if square:
                    for h in (0, 1):
                        arrived(halves(flip(p, 3), bs, h), ag_r.at[3 + h, bs])
                if pair % 128 == 0:
                    multiply(zz * pair, pair)

    for t in range(nz + 3):
        stage_line(t)
        stage_peer(t - 1)
        stage_diagonal(t - 2)
        stage_multiply(t - 3)
    if pair % 128 != 0:
        tile = math.lcm(pair, 128)

        @pl.loop(0, depth // tile)
        def _(i):
            multiply(i * tile, tile)

    for q in range(n_pol):
        merged_out[:, q * cw:(q + 1) * cw] = mg[q, pl.ds(pl.multiple_of(b * rows, 16), rows), :]

    for cond, make in sends:
        if cond is None:
            make().wait_send()
        else:
            @pl.when(cond)
            def _(make=make):
                make().wait_send()


def on_device(n_pol, n_zero, acts, cotan, advantage, merge_ratio, weight, anchor, init):
    tokens, depth = acts.shape[1:]
    rows, width = init.shape
    nz, cw = n_zero // 2, width // n_pol
    dma = pltpu.SemaphoreType.DMA
    vmem = pl.BlockSpec(memory_space=pltpu.VMEM)
    smem = pl.BlockSpec(memory_space=pltpu.SMEM)
    lanes = max(n_pol, 5)
    anchor_new, merged, result = pl.pallas_call(
        functools.partial(kernel, n_pol, n_zero, tokens * n_zero),
        out_shape=(
            jax.ShapeDtypeStruct((rows, width), F32),
            jax.ShapeDtypeStruct((rows, width), BF16),
            jax.ShapeDtypeStruct((tokens, width), F32),
        ),
        in_specs=[vmem, vmem, smem, smem, vmem, vmem, vmem],
        out_specs=(vmem, vmem, vmem),
        scratch_shapes=[
            pltpu.VMEM((tokens, width), BF16),
            pltpu.VMEM((depth, width), BF16),
            pltpu.VMEM((nz, rows, width), BF16),
            pltpu.VMEM((nz - 1, rows, width), BF16),
            pltpu.VMEM((nz - 1, rows, width), BF16),
            pltpu.VMEM((SUB, width), F32),
            pltpu.VMEM((n_pol, rows, cw), BF16),
            pltpu.VMEM((n_pol - 1, rows, cw), BF16),
            pltpu.VMEM((rows, cw), F32),
            pltpu.VMEM((n_pol, depth, cw), BF16),
            pltpu.VMEM((8, width), F32),
            pltpu.VMEM((8, cw), F32),
            pltpu.VMEM((n_zero, 2, 8, 128), F32),
            pltpu.VMEM((n_pol, 2, 8, 128), F32),
            dma((nz,)), dma((nz,)),
            dma((nz - 1, CHUNKS)), dma((nz - 1, CHUNKS)),
            dma((nz - 1, CHUNKS)), dma((nz - 1, CHUNKS)),
            dma((n_pol - 1, CHUNKS)), dma((n_pol - 1, CHUNKS)),
            dma((n_zero,)), dma((n_zero,)),
            dma((n_pol,)), dma((n_pol,)),
            dma((lanes, n_zero)), dma((2, nz)), dma((lanes, nz)), dma((lanes, nz)), dma((2, nz)),
        ],
        compiler_params=pltpu.CompilerParams(
            collective_id=0, has_side_effects=True, vmem_limit_bytes=63 * 1024 * 1024
        ),
        cost_estimate=pl.CostEstimate(
            flops=4 * tokens * depth * width, bytes_accessed=24 * 1024 * 1024, transcendentals=0
        ),
    )(acts[0], cotan[0], advantage, merge_ratio, weight[0], anchor[0], init)
    return anchor_new[None], merged, result[None]


def solution(mesh):
    placed = (
        P("policy", "zero", None),
        P("policy", "zero", None),
        P("policy", "zero"),
        P(),
        P("policy", "zero", None),
        P("policy", "zero", None),
        P("zero", None),
    )
    return jax.shard_map(
        functools.partial(on_device, mesh.shape["policy"], mesh.shape["zero"]),
        mesh=mesh,
        in_specs=placed,
        out_specs=(P("policy", "zero", None), P("zero", None), P("policy", "zero", None)),
        check_vma=False,
    )
```

time: 367 us -> 186 us (0.51)
  waiting for transfers between devices: 256 us -> 0 us
  Pallas kernels: 0 us -> 178 us
  blocking collectives: 26.6 us -> 0 us
  matrix products: 23.4 us -> 0 us
  local copies, waits for them, and re-layouts: 29.1 us -> 6.02 us
  between operations: 17.2 us -> 0.66 us
  other arithmetic: 13.5 us -> 0 us
    pallas_call x0 -> x1, Pallas kernels: none -> 178 us  [on_device(): pl.pallas_call(functools.partial(kernel, n_pol, n_zero, tokens * n_zero),...]
    unnamed x4 -> x0, waiting for transfers between devices: 93 us -> none
    all_gather x1 -> x0, waiting for transfers between devices: 86.1 us -> none  [on_device(): lax.all_gather(merged, 'zero', axis=0, tiled=True)]
    psum x1 -> x0, waiting for transfers between devices: 76.8 us -> none  [on_device(): mixed = lax.psum(term, 'policy')]
    psum x2 -> x0, blocking collectives: 26.6 us -> none  [the longest x1 17 us: on_device(): norm_sq = lax.psum(jnp.sum(task * task), 'zero')]
    dot_general x2 -> x0, matrix products: 23.4 us -> none  [the longest x1 12.4 us: on_device(): lax.dot_general(acts_local, scaled, (((0,), (0,)), ((), ())), preferred_e...]
    unnamed x14 -> x7, local copies, waits for them, and re-layouts: 28.5 us -> 6.02 us
    reduce_sum x3 -> x0, other arithmetic: 9.72 us -> none  [the longest x1 6.11 us: on_device(): norm_sq = lax.psum(jnp.sum(task * task), 'zero')]
  transfers between devices with their start and end apart: 3 -> 0, of which waited for: 3 -> 0; matrix products, arithmetic and copies ran while one was open for 2% -> 0% of each run, Pallas kernels for 0% -> 0%
where the time goes in v1:
time: 186 us; the launch traced here: 185 us
  Pallas kernels  178 us (96%)
  local copies, waits for them, and re-layouts  6.02 us (3%)
    pallas_call x1, Pallas kernels, on_device(): pl.pallas_call(functools.partial(kernel, n_pol, n_zero, tokens * n_zero),...  178 us
    unnamed x7, local copies, waits for them, and re-layouts  6.02 us

profile of v1, /device:TPU:0, one launch (start us, length us, event | category | flops | bytes accessed | tf_op | source)
XLA Modules:
  0.0 184.9 jit_solution(10899755130626880055)
XLA Ops:
  0.6 178.2 %shard_map.94 = (f32[576,1024]{1,0:T(8,128)}, bf16[576,1024]{1,0:T(8,128)(2,1)}, f32[640,1024]{1,0:T(8,128)}) custom-call(bf16[640,4608]{1,0:T(8,128)(2,1)} %bitcast.8, bf16[640,1024]{1,0:T(8,128)(2,1)} %bitcast.10, s32[1,5]{1,0:T(1,128)} %adv.1, s32[4]{0:T(128)} %ratio.1, bf16[576,1024]{1,0:T(8,128)(2,1)} %bitcast.11, f32[576,1024]{1,0:T(8,128)} %bitcast.9, ...), custom_call_target="tpu_custom_call" | custom-call | flops 12079595520 | bytes 25165824 | tf_op jit(solution)/shard_map/pallas_call | solution.py:401
  178.9 0.0 copy-start.1
  178.9 0.0 copy-start
  178.9 3.5 %copy.13 = f32[1,576,1024]{2,1,0:T(8,128)} copy(f32[1,576,1024]{2,1,0:T(8,128)} %bitcast.7) | data formatting | bytes 4718592
  182.4 0.0 copy-done.1
  182.4 1.0 copy.14
  183.4 0.0 copy-done
  183.4 1.5 copy.15
Async XLA Ops:
  178.9 3.5 %copy-start.1 = (bf16[576,1024]{1,0:T(8,128)(2,1)S(1)}, bf16[576,1024]{1,0:T(8,128)(2,1)}, u32[]{:S(2)}) copy-start(bf16[576,1024]{1,0:T(8,128)(2,1)} %get-tuple-element.13) | copy-start | bytes 3538948
  178.9 4.5 %copy-start = (f32[640,1024]{1,0:T(8,128)S(1)}, f32[640,1024]{1,0:T(8,128)}, u32[]{:S(2)}) copy-start(f32[640,1024]{1,0:T(8,128)} %get-tuple-element.8) | copy-start | bytes 7864324

commit v2 on v1

--- a/solution.py
+++ b/solution.py
@@ -93,62 +93,73 @@
         make().start()
         sends.append((None, make))
 
+    def sib_wait(d):
+        remote(sib.at[d], sib.at[d], sib_s.at[d], sib_r.at[d], zero=other).wait_recv()
+
+    ends = jnp.logical_or(z == 0, z == nz - 1)
+
+    def relay(i, k, who):
+        for (d, here, end, recv, r_sem, s_sem, slot, step) in (
+            (nz - 1 - i, z < nz - 1 - i, z == 0, up, up_r, up_s, nz - 2 - i, 2),
+            (i, z > i, z == nz - 1, dn, dn_r, dn_s, i, -2),
+        ):
+            mine = pl.ds(k * R, R)
+
+            def make(k, i_back=0, d=d, slot=slot, step=step, recv=recv, s_sem=s_sem, r_sem=r_sem):
+                dd, at = (d + i_back, slot + i_back) if step > 0 else (d - i_back, slot - i_back)
+                src = part.at[pl.ds(pl.multiple_of(dd * pair + c * rows + k * R, 16), R), :]
+                return remote(
+                    src, recv.at[at, pl.ds(k * R, R), :], s_sem.at[at, k], r_sem.at[at, k], zero=b + step
+                )
+
+            def add(with_recv):
+                @pl.loop(0, R // SUB)
+                def _(t):
+                    own = pl.ds(pl.multiple_of(d * pair + c * rows + k * R + t * SUB, SUB), SUB)
+                    at = pl.ds(pl.multiple_of(k * R + t * SUB, SUB), SUB)
+                    acc = part[own, :].astype(F32) + sib[d, at, :].astype(F32)
+                    if with_recv:
+                        acc = acc + recv[slot, at, :].astype(F32)
+                    part[own, :] = acc.astype(BF16)
+
+            if who == "ends":
+                @pl.when(jnp.logical_and(here, end))
+                def _():
+                    if k == 0:
+                        sib_wait(d)
+                    add(False)
+                    if i > 0:
+                        make(k, 1).wait_send()
+                    make(k).start()
+            else:
+                @pl.when(jnp.logical_and(here, jnp.logical_not(end)))
+                def _():
+                    if k == 0:
+                        sib_wait(d)
+                    remote(
+                        recv.at[slot, mine, :], recv.at[slot, mine, :], s_sem.at[slot, k], r_sem.at[slot, k], zero=b
+                    ).wait_recv()
+                    add(True)
+                    make(k).start()
+                sends.append((jnp.logical_and(here, jnp.logical_or(jnp.logical_not(end), i == nz - 2)),
+                              functools.partial(make, k)))
+
     order = []
     for i in range((nz + 1) // 2):
         order += [nz - 1 - i] + ([i] if i != nz - 1 - i else [])
+    upper = (2 * z) // nz
+    order = [d + upper * (nz - 1 - 2 * d) for d in order]
     if pair % T == 0:
-        for d in order:
+        for n, d in enumerate(order):
             tiles(d * pair, pair // T)
             to_sibling(d)
+            if n == 1:
+                relay(0, 0, "ends")
     else:
         tiles(0, depth // T)
         for d in order:
             to_sibling(d)
-
-    def sib_wait(d):
-        remote(sib.at[d], sib.at[d], sib_s.at[d], sib_r.at[d], zero=other).wait_recv()
-
-    def relay(k):
-        for i in range(nz - 1):
-            for (d, here, end, first_, recv, r_sem, s_sem, slot, step) in (
-                (nz - 1 - i, z < nz - 1 - i, z == 0, 0, up, up_r, up_s, nz - 2 - i, 2),
-                (i, z > i, z == nz - 1, nz - 1, dn, dn_r, dn_s, i, -2),
-            ):
-                mine = pl.ds(k * R, R)
-
-                def make(d=d, recv=recv, r_sem=r_sem, s_sem=s_sem, slot=slot, step=step, k=k, i=i, mine=mine):
-                    src = part.at[pl.ds(pl.multiple_of(d * pair + c * rows + k * R, 16), R), :]
-                    return remote(
-                        src, recv.at[slot, mine, :], s_sem.at[slot, k], r_sem.at[slot, k], zero=b + step
-                    )
-
-                def add(with_recv, d=d, recv=recv, slot=slot):
-                    @pl.loop(0, R // SUB)
-                    def _(t):
-                        own = pl.ds(pl.multiple_of(d * pair + c * rows + k * R + t * SUB, SUB), SUB)
-                        at = pl.ds(pl.multiple_of(k * R + t * SUB, SUB), SUB)
-                        acc = part[own, :].astype(F32) + sib[d, at, :].astype(F32)
-                        if with_recv:
-                            acc = acc + recv[slot, at, :].astype(F32)
-                        part[own, :] = acc.astype(BF16)
-
-                if k == 0:
-                    @pl.when(here)
-                    def _():
-                        sib_wait(d)
-
-                @pl.when(jnp.logical_and(here, end))
-                def _():
-                    add(False)
-
-                @pl.when(jnp.logical_and(here, jnp.logical_not(end)))
-                def _():
-                    remote(
-                        recv.at[slot, mine, :], recv.at[slot, mine, :], s_sem.at[slot, k], r_sem.at[slot, k], zero=b
-                    ).wait_recv()
-                    add(True)
-
-                post(here, make)
+        relay(0, 0, "ends")
 
     share = jnp.full((8, 128), ratio[p].astype(F32), F32)
     whole = 0
@@ -196,13 +207,14 @@
                 ubuf[q, at, :] = term[:, q * cw:(q + 1) * cw]
 
         for j in range(1, n_pol):
-            def make(j=j):
-                q = flip(p, j)
-                return remote(
-                    ubuf.at[q, mine, :], prec.at[j - 1, mine, :], pol_s.at[j - 1, k], pol_r.at[j - 1, k], policy=q
-                )
-            make().start()
-            sends.append((None, make))
+            to_policy(k, j).start()
+
+    def to_policy(k, j):
+        mine = pl.ds(k * R, R)
+        return remote(
+            ubuf.at[flip(p, j), mine, :], prec.at[j - 1, mine, :], pol_s.at[j - 1, k], pol_r.at[j - 1, k],
+            policy=flip(p, j)
+        )
 
     columns = pl.ds(pl.multiple_of(p * cw, 128), cw)
 
@@ -223,15 +235,23 @@
             sq = acc * acc
             msq[...] += sq[:8] + sq[8:]
 
+    turn = jnp.where(ends, min(1, nz - 2), jnp.minimum(jnp.maximum(nz - 1 - z, z) + 1, nz - 2))
+    for i in range(nz - 1):
+        for k in range(CHUNKS):
+            if i or k:
+                relay(i, k, "ends")
+            relay(i, k, "others")
+
+            @pl.when(turn == i)
+            def _():
+                final(k)
+                if k:
+                    mix(k - 1)
+                if k == CHUNKS - 1:
+                    mix(k)
     for k in range(CHUNKS):
-        relay(k)
-        if k >= 1:
-            final(k - 1)
-        if k >= 2:
-            mix(k - 2)
-    final(CHUNKS - 1)
-    for k in range(max(CHUNKS - 2, 0), CHUNKS):
-        mix(k)
+        for j in range(1, n_pol):
+            sends.append((None, functools.partial(to_policy, k, j)))
 
     ztile[b, 0] = jnp.full((8, 128), jnp.sum(nsq[...]), F32)
     ztile[b, 1] = jnp.full((8, 128), jnp.sum(msq[...]), F32)

time: 186 us -> 183 us (0.984)
  Pallas kernels: 178 us -> 174 us
    pallas_call x1, Pallas kernels: 178 us -> 174 us  [on_device(): pl.pallas_call(functools.partial(kernel, n_pol, n_zero, tokens * n_zero),...]
where the time goes in v2:
time: 183 us; the launch traced here: 181 us
  Pallas kernels  174 us (95%)
  local copies, waits for them, and re-layouts  6.02 us (3%)
    pallas_call x1, Pallas kernels, on_device(): pl.pallas_call(functools.partial(kernel, n_pol, n_zero, tokens * n_zero),...  174 us
    unnamed x7, local copies, waits for them, and re-layouts  6.02 us

profile of v2, /device:TPU:0, one launch (start us, length us, event | category | flops | bytes accessed | tf_op | source)
XLA Modules:
  0.0 180.8 jit_solution(5859696550824009455)
XLA Ops:
  0.6 174.1 %shard_map.94 = (f32[576,1024]{1,0:T(8,128)}, bf16[576,1024]{1,0:T(8,128)(2,1)}, f32[640,1024]{1,0:T(8,128)}) custom-call(bf16[640,4608]{1,0:T(8,128)(2,1)} %bitcast.8, bf16[640,1024]{1,0:T(8,128)(2,1)} %bitcast.10, s32[1,5]{1,0:T(1,128)} %adv.1, s32[4]{0:T(128)} %ratio.1, bf16[576,1024]{1,0:T(8,128)(2,1)} %bitcast.11, f32[576,1024]{1,0:T(8,128)} %bitcast.9, ...), custom_call_target="tpu_custom_call" | custom-call | flops 12079595520 | bytes 25165824 | tf_op jit(solution)/shard_map/pallas_call | solution.py:421
  174.8 0.0 copy-start.1
  174.8 0.0 copy-start
  174.8 3.5 %copy.13 = f32[1,576,1024]{2,1,0:T(8,128)} copy(f32[1,576,1024]{2,1,0:T(8,128)} %bitcast.7) | data formatting | bytes 4718592
  178.3 0.0 copy-done.1
  178.3 1.0 copy.14
  179.3 0.0 copy-done
  179.3 1.5 copy.15
Async XLA Ops:
  174.8 3.5 %copy-start.1 = (bf16[576,1024]{1,0:T(8,128)(2,1)S(1)}, bf16[576,1024]{1,0:T(8,128)(2,1)}, u32[]{:S(2)}) copy-start(bf16[576,1024]{1,0:T(8,128)(2,1)} %get-tuple-element.13) | copy-start | bytes 3538948
  174.8 4.5 %copy-start = (f32[640,1024]{1,0:T(8,128)S(1)}, f32[640,1024]{1,0:T(8,128)}, u32[]{:S(2)}) copy-start(f32[640,1024]{1,0:T(8,128)} %get-tuple-element.8) | copy-start | bytes 7864324

commit v3 on v2

--- a/solution.py
+++ b/solution.py
@@ -37,8 +37,8 @@
     n_pol, n_zero, total_tokens,
     acts, cotan, adv, ratio, weight, anchor, init,
     anchor_out, merged_out, result,
-    scaled, part, sib, up, dn, grad, ubuf, prec, mixed, mg, nsq, msq, ztile, ptile,
-    sib_s, sib_r, up_s, up_r, dn_s, dn_r, pol_s, pol_r, zs_s, zs_r, ps_s, ps_r, ag_r, line_s, peer_s, core_s, relay_s,
+    scaled, part, sib, up, dn, grad, ubuf, prec, base, mg, second, nsq, msq, ztile, ptile,
+    sib_s, sib_r, up_s, up_r, dn_s, dn_r, pol_s, pol_r, zs_s, zs_r, ps_s, ps_r, ag_r, line_s, peer_s, core_s, relay_s, load_s,
 ):
     p = lax.axis_index("policy")
     b = lax.axis_index("zero")
@@ -64,17 +64,154 @@
     for j in range(1, n_pol):
         pl.semaphore_signal(barrier, inc=1, device_id={"policy": flip(p, j)}, device_id_type=MESH)
 
+    load = pltpu.make_async_copy(cotan, scaled, load_s.at[0])
+    load_anchor = pltpu.make_async_copy(anchor, anchor_out, load_s.at[1])
+    load.start()
+    load_anchor.start()
+    load.wait()
     for s in range(adv.shape[1]):
         level = adv[0, s].astype(F32) * 0.25
 
         @pl.loop(0, SEQ // SUB)
         def _(i):
             at = pl.ds(pl.multiple_of(s * SEQ + i * SUB, SUB), SUB)
-            scaled[at, :] = (cotan[at, :].astype(F32) * level).astype(BF16)
+            scaled[at, :] = (scaled[at, :].astype(F32) * level).astype(BF16)
 
     nsq[...] = jnp.zeros_like(nsq)
     msq[...] = jnp.zeros_like(msq)
+    result[...] = jnp.zeros_like(result)
+    second[...] = jnp.zeros_like(second)
+    square = n_pol == 4
+    direct = (1, 2) if square else tuple(range(1, n_pol))
+    half = rows // 2
+
+    def piece(w, q, block):
+        return (base, mg)[w].at[q, pl.ds(pl.multiple_of(block * rows, 16), rows), :]
+
+    def halves(w, q, block, h):
+        return (base, mg)[w].at[q, pl.ds(pl.multiple_of(block * rows + h * half, 16), half), :]
+
+    def arrived(ref, sem):
+        remote(ref, ref, sem, sem, zero=b).wait_recv()
+
+    def offsets(t):
+        if t < 0 or t >= nz:
+            return []
+        return [0] if t == 0 else [-t, t]
+
+    def valid(o, kind):
+        zz = z + o
+        ok = jnp.logical_and(zz >= 0, zz < nz)
+        outer = jnp.logical_or(zz == 0, zz == nz - 1)
+        if kind == "outer":
+            return jnp.logical_and(ok, outer)
+        if kind == "inner":
+            return jnp.logical_and(ok, jnp.logical_not(outer))
+        return ok
+
+    def stage_line(t, w, kind):
+        for o in offsets(t):
+            ok = valid(o, kind)
+            zz = z + o
+            bb = 2 * zz + c
+            if t:
+                @pl.when(ok)
+                def _():
+                    arrived(piece(w, p, bb), ag_r.at[w, 0, bb])
+            if o <= 0:
+                post(jnp.logical_and(ok, z < nz - 1), lambda zz=zz, bb=bb: remote(
+                    piece(w, p, bb), piece(w, p, bb), line_s.at[w, 0, zz], ag_r.at[w, 0, bb], zero=b + 2))
+            if o >= 0:
+                post(jnp.logical_and(ok, z > 0), lambda zz=zz, bb=bb: remote(
+                    piece(w, p, bb), piece(w, p, bb), line_s.at[w, 1, zz], ag_r.at[w, 0, bb], zero=b - 2))
+            for j in direct:
+                post(ok, lambda zz=zz, bb=bb, j=j: remote(
+                    piece(w, p, bb), piece(w, p, bb), peer_s.at[w, j, zz], ag_r.at[w, j, bb], policy=flip(p, j)))
+            post(ok, lambda zz=zz, bb=bb: remote(
+                piece(w, p, bb), piece(w, p, bb), core_s.at[w, 0, zz], ag_r.at[w, 0, bb], zero=other))
+
+    def stage_peer(t, w, kind):
+        for o in offsets(t):
+            ok = valid(o, kind)
+            zz = z + o
+            bb = 2 * zz + c
+            for j in direct:
+                q = flip(p, j)
+
+                @pl.when(ok)
+                def _(j=j, q=q):
+                    arrived(piece(w, q, bb), ag_r.at[w, j, bb])
+                if square:
+                    post(ok, lambda zz=zz, bb=bb, j=j, q=q: remote(
+                        halves(w, q, bb, j - 1), halves(w, q, bb, j - 1), relay_s.at[w, j - 1, zz], ag_r.at[w, 2 + j, bb],
+                        policy=flip(p, 3 - j)))
+                post(ok, lambda zz=zz, bb=bb, j=j, q=q: remote(
+                    piece(w, q, bb), piece(w, q, bb), core_s.at[w, j, zz], ag_r.at[w, j, bb], zero=other))
+
+    def stage_diagonal(t, w, kind):
+        if not square:
+            return
+        for o in offsets(t):
+            ok = valid(o, kind)
+            zz = z + o
+            bb = 2 * zz + c
+            q = flip(p, 3)
+            for h in (0, 1):
+                @pl.when(ok)
+                def _(h=h):
+                    arrived(halves(w, q, bb, h), ag_r.at[w, 3 + h, bb])
+                post(ok, lambda zz=zz, bb=bb, h=h, q=q: remote(
+                    halves(w, q, bb, h), halves(w, q, bb, h), core_s.at[w, 3 + h, zz], ag_r.at[w, 3 + h, bb], zero=other))
+
+    def multiply(w, first, count):
+        k_at = pl.ds(pl.multiple_of(first, 128), count)
+        src, out = (base, mg)[w], (result, second)[w]
+
+        @pl.loop(0, n_pol)
+        def _(q):
+            n_at = pl.ds(pl.multiple_of(q * cw, 128), cw)
+            out[:, n_at] += jnp.dot(acts[:, k_at], src[q, k_at, :], preferred_element_type=F32)
+
+    def stage_multiply(t, w, kind):
+        for o in offsets(t):
+            zz = z + o
+            bs = 2 * zz + 1 - c
+
+            @pl.when(valid(o, kind))
+            def _():
+                arrived(piece(w, p, bs), ag_r.at[w, 0, bs])
+                for j in direct:
+                    arrived(piece(w, flip(p, j), bs), ag_r.at[w, j, bs])
+                if square:
+                    for h in (0, 1):
+                        arrived(halves(w, flip(p, 3), bs, h), ag_r.at[w, 3 + h, bs])
+
+        if pair % 128 == 0 and offsets(t):
+            @pl.loop(0, 1 + (t > 0))
+            def _(i):
+                o = 2 * t * i - t
+
+                @pl.when(valid(o, kind))
+                def _():
+                    multiply(w, (z + o) * pair, pair)
+
+    def gather(t, w, kind):
+        stage_line(t, w, kind)
+        stage_peer(t - 1, w, kind)
+        stage_diagonal(t - 2, w, kind)
+        stage_multiply(t - 3, w, kind)
+
+    last = nz + 2
+    columns = pl.ds(pl.multiple_of(p * cw, 128), cw)
+
+    @pl.loop(0, rows // SUB)
+    def _(t):
+        at = pl.ds(pl.multiple_of(t * SUB, SUB), SUB)
+        own = pl.ds(pl.multiple_of(b * rows + t * SUB, SUB), SUB)
+        base[p, own, :] = init[at, columns]
+
     pl.semaphore_wait(barrier, n_zero - 1 + n_pol - 1)
+    gather(0, 0, None)
 
     T = 384
 
@@ -161,6 +298,7 @@
             to_sibling(d)
         relay(0, 0, "ends")
 
+    load_anchor.wait()
     share = jnp.full((8, 128), ratio[p].astype(F32), F32)
     whole = 0
     for q in range(n_pol):
@@ -198,7 +336,7 @@
                 grad[...] += dn[z, at, :].astype(F32)
 
             updated = weight[at, :].astype(F32) - factor * grad[...]
-            anchor_out[at, :] = DECAY * anchor[at, :] + (1.0 - DECAY) * updated
+            anchor_out[at, :] = DECAY * anchor_out[at, :] + (1.0 - DECAY) * updated
             task = updated - init[at, :].astype(F32)
             sq = task * task
             nsq[...] += sq[:8] + sq[8:]
@@ -230,8 +368,8 @@
             acc = ubuf[p, at, :].astype(F32)
             for j in range(1, n_pol):
                 acc = acc + prec[j - 1, at, :].astype(F32)
+            mg[p, pl.ds(pl.multiple_of(b * rows + k * R + t * SUB, SUB), SUB), :] = acc.astype(BF16)
             acc = acc - init[at, columns].astype(F32)
-            mixed[at, :] = acc
             sq = acc * acc
             msq[...] += sq[:8] + sq[8:]
 
@@ -249,9 +387,19 @@
                     mix(k - 1)
                 if k == CHUNKS - 1:
                     mix(k)
+
+            n = i * CHUNKS + k
+            if 1 <= n + 1 <= last:
+                gather(n + 1, 0, None)
+            m = n - (min(1, nz - 2) * CHUNKS + CHUNKS - 1)
+            if 0 <= m <= last:
+                gather(m, 1, "outer")
     for k in range(CHUNKS):
         for j in range(1, n_pol):
             sends.append((None, functools.partial(to_policy, k, j)))
+
+    done = n
+    gather(0, 1, "inner")
 
     ztile[b, 0] = jnp.full((8, 128), jnp.sum(nsq[...]), F32)
     ztile[b, 1] = jnp.full((8, 128), jnp.sum(msq[...]), F32)
@@ -260,7 +408,10 @@
             return remote(ztile.at[b], ztile.at[b], zs_s.at[j], zs_r.at[j], zero=lax.rem(b + j, n_zero))
         make().start()
         sends.append((None, make))
-    result[...] = jnp.zeros_like(result)
+    for n in range(done + 2, last + 1):
+        gather(n, 0, None)
+    gather(m + 1, 1, "outer")
+    gather(1, 1, "inner")
     for j in range(1, n_zero):
         ref = ztile.at[lax.rem(b + n_zero - j, n_zero)]
         remote(ref, ref, zs_s.at[j], zs_r.at[j], zero=b).wait_recv()
@@ -281,125 +432,31 @@
         mixed_sq = mixed_sq + ptile[q, 1]
     scale = (target / jnp.sqrt(mixed_sq))[0:1, 0:1]
 
+    for n in range(2, last + 1):
+        gather(n, 1, "inner")
+        if m + n <= last:
+            gather(m + n, 1, "outer")
+    if pair % 128 != 0:
+        tile = math.lcm(pair, 128)
+        for w in (0, 1):
+            @pl.loop(0, depth // tile)
+            def _(i):
+                multiply(w, i * tile, tile)
+
+    @pl.loop(0, result.shape[0] // SUB)
+    def _(t):
+        at = pl.ds(pl.multiple_of(t * SUB, SUB), SUB)
+        result[at, :] = (1.0 - scale) * result[at, :] + scale * second[at, :]
+
     @pl.loop(0, rows // SUB)
     def _(t):
         at = pl.ds(pl.multiple_of(t * SUB, SUB), SUB)
         own = pl.ds(pl.multiple_of(b * rows + t * SUB, SUB), SUB)
-        mg[p, own, :] = (init[at, columns].astype(F32) + mixed[at, :] * scale).astype(BF16)
-
-    square = n_pol == 4
-    direct = (1, 2) if square else tuple(range(1, n_pol))
-    half = rows // 2
-
-    def piece(q, block):
-        return mg.at[q, pl.ds(pl.multiple_of(block * rows, 16), rows), :]
-
-    def halves(q, block, h):
-        return mg.at[q, pl.ds(pl.multiple_of(block * rows + h * half, 16), half), :]
-
-    def arrived(ref, sem):
-        remote(ref, ref, sem, sem, zero=b).wait_recv()
-
-    def offsets(t):
-        if t < 0 or t >= nz:
-            return []
-        return [0] if t == 0 else [-t, t]
-
-    def valid(o):
-        return jnp.logical_and(z + o >= 0, z + o < nz)
-
-    def stage_line(t):
-        for o in offsets(t):
-            ok = valid(o)
-            zz = z + o
-            bb = 2 * zz + c
-            if t:
-                @pl.when(ok)
-                def _():
-                    arrived(piece(p, bb), ag_r.at[0, bb])
-            if o <= 0:
-                post(jnp.logical_and(ok, z < nz - 1), lambda zz=zz, bb=bb: remote(
-                    piece(p, bb), piece(p, bb), line_s.at[0, zz], ag_r.at[0, bb], zero=b + 2))
-            if o >= 0:
-                post(jnp.logical_and(ok, z > 0), lambda zz=zz, bb=bb: remote(
-                    piece(p, bb), piece(p, bb), line_s.at[1, zz], ag_r.at[0, bb], zero=b - 2))
-            for j in direct:
-                post(ok, lambda zz=zz, bb=bb, j=j: remote(
-                    piece(p, bb), piece(p, bb), peer_s.at[j, zz], ag_r.at[j, bb], policy=flip(p, j)))
-            post(ok, lambda zz=zz, bb=bb: remote(
-                piece(p, bb), piece(p, bb), core_s.at[0, zz], ag_r.at[0, bb], zero=other))
-
-    def stage_peer(t):
-        for o in offsets(t):
-            ok = valid(o)
-            zz = z + o
-            bb = 2 * zz + c
-            for j in direct:
-                q = flip(p, j)
-
-                @pl.when(ok)
-                def _(j=j, q=q):
-                    arrived(piece(q, bb), ag_r.at[j, bb])
-                if square:
-                    post(ok, lambda zz=zz, bb=bb, j=j, q=q: remote(
-                        halves(q, bb, j - 1), halves(q, bb, j - 1), relay_s.at[j - 1, zz], ag_r.at[2 + j, bb],
-                        policy=flip(p, 3 - j)))
-                post(ok, lambda zz=zz, bb=bb, j=j, q=q: remote(
-                    piece(q, bb), piece(q, bb), core_s.at[j, zz], ag_r.at[j, bb], zero=other))
-
-    def stage_diagonal(t):
-        if not square:
-            return
-        for o in offsets(t):
-            ok = valid(o)
-            zz = z + o
-            bb = 2 * zz + c
-            q = flip(p, 3)
-            for h in (0, 1):
-                @pl.when(ok)
-                def _(h=h):
-                    arrived(halves(q, bb, h), ag_r.at[3 + h, bb])
-                post(ok, lambda zz=zz, bb=bb, h=h, q=q: remote(
-                    halves(q, bb, h), halves(q, bb, h), core_s.at[3 + h, zz], ag_r.at[3 + h, bb], zero=other))
-
-    def multiply(first, count):
-        k_at = pl.ds(pl.multiple_of(first, 128), count)
-
-        @pl.loop(0, n_pol)
-        def _(q):
-            n_at = pl.ds(pl.multiple_of(q * cw, 128), cw)
-            result[:, n_at] += jnp.dot(acts[:, k_at], mg[q, k_at, :], preferred_element_type=F32)
-
-    def stage_multiply(t):
-        for o in offsets(t):
-            zz = z + o
-            bs = 2 * zz + 1 - c
-
-            @pl.when(valid(o))
-            def _():
-                arrived(piece(p, bs), ag_r.at[0, bs])
-                for j in direct:
-                    arrived(piece(flip(p, j), bs), ag_r.at[j, bs])
-                if square:
-                    for h in (0, 1):
-                        arrived(halves(flip(p, 3), bs, h), ag_r.at[3 + h, bs])
-                if pair % 128 == 0:
-                    multiply(zz * pair, pair)
-
-    for t in range(nz + 3):
-        stage_line(t)
-        stage_peer(t - 1)
-        stage_diagonal(t - 2)
-        stage_multiply(t - 3)
-    if pair % 128 != 0:
-        tile = math.lcm(pair, 128)
-
-        @pl.loop(0, depth // tile)
-        def _(i):
-            multiply(i * tile, tile)
-
-    for q in range(n_pol):
-        merged_out[:, q * cw:(q + 1) * cw] = mg[q, pl.ds(pl.multiple_of(b * rows, 16), rows), :]
+        for q in range(n_pol):
+            start = init[at, q * cw:(q + 1) * cw].astype(F32)
+            merged_out[at, q * cw:(q + 1) * cw] = (
+                start + (mg[q, own, :].astype(F32) - start) * scale
+            ).astype(BF16)
 
     for cond, make in sends:
         if cond is None:
@@ -416,6 +473,7 @@
     nz, cw = n_zero // 2, width // n_pol
     dma = pltpu.SemaphoreType.DMA
     vmem = pl.BlockSpec(memory_space=pltpu.VMEM)
+    anywhere = pl.BlockSpec(memory_space=pl.ANY)
     smem = pl.BlockSpec(memory_space=pltpu.SMEM)
     lanes = max(n_pol, 5)
     anchor_new, merged, result = pl.pallas_call(
@@ -425,7 +483,7 @@
             jax.ShapeDtypeStruct((rows, width), BF16),
             jax.ShapeDtypeStruct((tokens, width), F32),
         ),
-        in_specs=[vmem, vmem, smem, smem, vmem, vmem, vmem],
+        in_specs=[vmem, anywhere, smem, smem, vmem, anywhere, vmem],
         out_specs=(vmem, vmem, vmem),
         scratch_shapes=[
             pltpu.VMEM((tokens, width), BF16),
@@ -436,8 +494,9 @@
             pltpu.VMEM((SUB, width), F32),
             pltpu.VMEM((n_pol, rows, cw), BF16),
             pltpu.VMEM((n_pol - 1, rows, cw), BF16),
-            pltpu.VMEM((rows, cw), F32),
             pltpu.VMEM((n_pol, depth, cw), BF16),
+            pltpu.VMEM((n_pol, depth, cw), BF16),
+            pltpu.VMEM((tokens, width), F32),
             pltpu.VMEM((8, width), F32),
             pltpu.VMEM((8, cw), F32),
             pltpu.VMEM((n_zero, 2, 8, 128), F32),
@@ -448,7 +507,7 @@
             dma((n_pol - 1, CHUNKS)), dma((n_pol - 1, CHUNKS)),
             dma((n_zero,)), dma((n_zero,)),
             dma((n_pol,)), dma((n_pol,)),
-            dma((lanes, n_zero)), dma((2, nz)), dma((lanes, nz)), dma((lanes, nz)), dma((2, nz)),
+            dma((2, lanes, n_zero)), dma((2, 2, nz)), dma((2, lanes, nz)), dma((2, lanes, nz)), dma((2, 2, nz)), dma((2,)),
         ],
         compiler_params=pltpu.CompilerParams(
             collective_id=0, has_side_effects=True, vmem_limit_bytes=63 * 1024 * 1024

time: 183 us -> 199 us (1.087); the launches traced: 181 us -> 199 us
  Pallas kernels: 174 us -> 192 us
    pallas_call x1, Pallas kernels: 174 us -> 192 us  [on_device(): pl.pallas_call(functools.partial(kernel, n_pol, n_zero, tokens * n_zero),...]
where the time goes in v3:
time: 199 us
  Pallas kernels  192 us (96%)
  local copies, waits for them, and re-layouts  6.02 us (3%)
    pallas_call x1, Pallas kernels, on_device(): pl.pallas_call(functools.partial(kernel, n_pol, n_zero, tokens * n_zero),...  192 us
    unnamed x7, local copies, waits for them, and re-layouts  6.02 us

profile of v3, /device:TPU:0, one launch (start us, length us, event | category | flops | bytes accessed | tf_op | source)
XLA Modules:
  0.0 198.9 jit_solution(5933955913818286470)
XLA Ops:
  0.6 192.2 %shard_map.94 = (f32[576,1024]{1,0:T(8,128)}, bf16[576,1024]{1,0:T(8,128)(2,1)}, f32[640,1024]{1,0:T(8,128)}) custom-call(bf16[640,4608]{1,0:T(8,128)(2,1)} %bitcast.8, bf16[640,1024]{1,0:T(8,128)(2,1)} %bitcast.10, s32[1,5]{1,0:T(1,128)} %adv.1, s32[4]{0:T(128)} %ratio.1, bf16[576,1024]{1,0:T(8,128)(2,1)} %bitcast.11, f32[576,1024]{1,0:T(8,128)} %bitcast.9, ...), custom_call_target="tpu_custom_call" | custom-call | flops 12079595520 | bytes 25165824 | tf_op jit(solution)/shard_map/pallas_call | solution.py:479
  192.9 0.0 copy-start.1
  192.9 0.0 copy-start
  192.9 3.5 %copy.13 = f32[1,576,1024]{2,1,0:T(8,128)} copy(f32[1,576,1024]{2,1,0:T(8,128)} %bitcast.7) | data formatting | bytes 4718592
  196.4 0.0 copy-done.1
  196.4 1.0 copy.14
  197.4 0.0 copy-done
  197.4 1.5 copy.15
Async XLA Ops:
  192.9 3.5 %copy-start.1 = (bf16[576,1024]{1,0:T(8,128)(2,1)S(1)}, bf16[576,1024]{1,0:T(8,128)(2,1)}, u32[]{:S(2)}) copy-start(bf16[576,1024]{1,0:T(8,128)(2,1)} %get-tuple-element.13) | copy-start | bytes 3538948
  192.9 4.5 %copy-start = (f32[640,1024]{1,0:T(8,128)S(1)}, f32[640,1024]{1,0:T(8,128)}, u32[]{:S(2)}) copy-start(f32[640,1024]{1,0:T(8,128)} %get-tuple-element.8) | copy-start | bytes 7864324
